TPU v7x, 32 devices: a whole 2x2x4 slice. The times are simulated.
32 devices in a mesh: gx: 2 (over x), gy: 4 (over y, core), gz: 4 (over z).
Axes of the slice: x: 2, y: 2, z: 4, core: 2. Of those that a mesh axis runs over, the one named last changes fastest.
Arguments:
- right_side: float32 [3, 16, 32, 32, 128], P(None, 'gx', 'gy', 'gz'), may hold values from -24 to 24
- stiffness: float32 [3, 16, 32, 32], P(None, 'gx', 'gy', 'gz'), may hold values from 0.25 to 4
- local_factor: bfloat16 [2, 4, 4, 2048, 2048], P('gx', 'gy', 'gz'), as said below
- basis: bfloat16 [2, 4, 4, 64, 1536], P('gx', 'gy', 'gz'), may hold values from -0.3125 to 0.3125
- coarse_map: int32 [2, 4, 4, 64], P('gx', 'gy', 'gz'), may hold values from 0 to 63, each once within a row
- margin_index: int32 [2, 4, 4, 512], P('gx', 'gy', 'gz'), may hold values from 0 to 1151, as said below
- coarse_inverse: bfloat16 [2048, 2048], P(('gx', 'gy', 'gz')), as said below
Outputs:
- solution: float32 [3, 16, 32, 32, 128], P(None, 'gx', 'gy', 'gz')
- residual_ratio: float32 [128], replicated
Inputs may be any that keep to these rules, and one draw needn't show every extreme that they name: `local_factor`: each subdomain's factor is zero above its diagonal. coarse_inverse is symmetric. `margin_index`: within each subdomain the 512 entries are distinct and increasing. `coarse_map`: each subdomain's entries are a permutation of 0 to 63.
All inputs are finite; a program needn't handle non-finite values.
Results may differ from a plain program's by a relative error of at most 0.0055.
Values may be sent and summed in bfloat16 or wider, within the bound.
A program may use at most 64 MiB of HBM per device.

v0:
```python
import jax
import jax.numpy as jnp
from jax import lax
from jax.sharding import PartitionSpec as P

EPSILON = 1e-06


def with_halo(block, sides, width):
    for axis, dim in sides:
        count = lax.axis_size(axis)
        forward = [(i, i + 1) for i in range(count - 1)]
        backward = [(target, source) for source, target in forward]
        low = lax.ppermute(
            lax.slice_in_dim(block, block.shape[dim] - width, None, axis=dim), axis, forward
        )
        high = lax.ppermute(lax.slice_in_dim(block, 0, width, axis=dim), axis, backward)
        block = jnp.concatenate([low, block, high], axis=dim)
    return block


def inner(left, right):
    return jnp.sum(left * right, axis=(0, 1, 2, 3))


def face_rows(padded):
    rhs_count = padded.shape[-1]
    slabs = [
        padded[:, 0, 1:-1, 1:-1],
        padded[:, -1, 1:-1, 1:-1],
        padded[:, 1:-1, 0, 1:-1],
        padded[:, 1:-1, -1, 1:-1],
        padded[:, 1:-1, 1:-1, 0],
        padded[:, 1:-1, 1:-1, -1],
    ]
    joined = jnp.concatenate([slab.reshape(slab.shape[0], -1, rhs_count) for slab in slabs], axis=1)
    return joined.reshape(-1, rhs_count)


def norm_sum(field):
    return lax.psum(inner(field, field), ("gx", "gy", "gz"))


def orthogonalize(mapped, previous):
    partials = jnp.stack([inner(mapped, vector) for vector in previous] + [inner(mapped, mapped)])
    totals = lax.psum(partials, ("gx", "gy", "gz"))
    coeffs = [totals[position] for position in range(len(previous))]
    remainder = mapped
    square = totals[-1]
    for weight_value, vector in zip(coeffs, previous):
        remainder = remainder - weight_value * vector
        square = square - weight_value * weight_value
    return (remainder, coeffs, jnp.sqrt(square + EPSILON))


def local(right_side, stiffness, local_factor, basis, coarse_map, margin_index, coarse_inverse):
    factor = local_factor.reshape(local_factor.shape[-2:])
    coarse_basis = basis.reshape(basis.shape[-2:])
    basis_count = coarse_basis.shape[0]
    coarse_ids = coarse_map.reshape(-1)
    margin_rows = margin_index.reshape(-1)
    placement_table = (
        coarse_ids[None, :] == lax.broadcasted_iota(jnp.int32, (basis_count, basis_count), 0)
    ).astype(jnp.float32)
    contract_first = (((0,), (0,)), ((), ()))

    def precondition(field):
        rounded = field.astype(jnp.bfloat16)
        padded = with_halo(rounded, (("gx", 1), ("gy", 2), ("gz", 3)), 1)
        own_rows = rounded.reshape(-1, rounded.shape[-1])
        extended = jnp.concatenate(
            [own_rows, jnp.take(face_rows(padded), margin_rows, axis=0)], axis=0
        )
        front_values = jnp.dot(factor, extended, preferred_element_type=jnp.float32).astype(
            jnp.bfloat16
        )
        back_sweep = lax.dot_general(
            factor, front_values, contract_first, preferred_element_type=jnp.float32
        )
        local_part = back_sweep[: own_rows.shape[0]]
        restricted = jnp.dot(coarse_basis, own_rows, preferred_element_type=jnp.float32)
        placed = jnp.dot(placement_table, restricted, precision=lax.Precision.HIGHEST).astype(
            jnp.bfloat16
        )
        solved = jnp.dot(
            coarse_inverse,
            lax.all_gather(placed, ("gx", "gy", "gz"), axis=0, tiled=True),
            preferred_element_type=jnp.float32,
        )
        solved = solved.astype(jnp.bfloat16)
        own_coarse = lax.dot_general(
            placement_table,
            solved.astype(jnp.float32),
            contract_first,
            precision=lax.Precision.HIGHEST,
        ).astype(jnp.bfloat16)
        coarse_part = lax.dot_general(
            coarse_basis, own_coarse, contract_first, preferred_element_type=jnp.float32
        )
        return (local_part + coarse_part).reshape(field.shape)

    def operate(field):
        padded = with_halo(field.astype(jnp.bfloat16), (("gx", 1), ("gy", 2), ("gz", 3)), 1).astype(
            field.dtype
        )
        beside = padded[:, 2:, 1:-1, 1:-1] + padded[:, :-2, 1:-1, 1:-1]
        beside = beside + padded[:, 1:-1, 2:, 1:-1] + padded[:, 1:-1, :-2, 1:-1]
        beside = beside + padded[:, 1:-1, 1:-1, 2:] + padded[:, 1:-1, 1:-1, :-2]
        return (6.0 + stiffness[..., None]) * field - beside

    start_norm = jnp.sqrt(norm_sum(right_side) + EPSILON)
    basis_one = right_side / start_norm
    search_one = precondition(basis_one)
    remainder, first_coeffs, norm_two = orthogonalize(operate(search_one), [basis_one])
    basis_two = remainder / norm_two
    search_two = precondition(basis_two)
    remainder, second_coeffs, norm_three = orthogonalize(
        operate(search_two), [basis_one, basis_two]
    )
    along_one = first_coeffs[0]
    cross_two = second_coeffs[0]
    along_two = second_coeffs[1]
    radius_one = jnp.sqrt(along_one * along_one + norm_two * norm_two)
    cosine_one = along_one / radius_one
    sine_one = norm_two / radius_one
    turned_one = cosine_one * cross_two + sine_one * along_two
    turned_two = cosine_one * along_two - sine_one * cross_two
    radius_two = jnp.sqrt(turned_two * turned_two + norm_three * norm_three)
    cosine_two = turned_two / radius_two
    sine_two = norm_three / radius_two
    coef_two = -cosine_two * sine_one * start_norm / radius_two
    coef_one = (cosine_one * start_norm - turned_one * coef_two) / radius_one
    solution = coef_one * search_one + coef_two * search_two
    return (solution, sine_one * sine_two)


def solution(mesh):
    return jax.shard_map(
        local,
        mesh=mesh,
        in_specs=(
            P(None, "gx", "gy", "gz", None),
            P(None, "gx", "gy", "gz"),
            P("gx", "gy", "gz", None, None),
            P("gx", "gy", "gz", None, None),
            P("gx", "gy", "gz", None),
            P("gx", "gy", "gz", None),
            P(("gx", "gy", "gz"), None),
        ),
        out_specs=(P(None, "gx", "gy", "gz", None), P()),
        check_vma=False,
    )
```

profile of v0, /device:TPU:0, one launch (start us, length us, event | category | flops | bytes accessed | tf_op | source)
XLA Modules:
  0.0 396.7 jit_solution(10328727986047043290)
XLA Ops:
  2.1 42.0 %psum.21 = f32[128]{0:T(128)S(1)} all-reduce(f32[128]{0:T(128)S(1)} %multiply_reduce_fusion.5), channel_id=1, replica_groups=mesh['gx'=2,'gy'=4,'gz'=4] {'gx','gy','gz'}, use_global_device_ids=true, to_apply=%region_1.0 | all-reduce | flops 128 | bytes 1024 | tf_op jit(solution)/shard_map/psum | solution.py:41
  46.6 4.5 %collective-permute-start = (bf16[3,1,8,8,128]{4,3,2,1,0:T(8,128)(2,1)S(1)}, bf16[3,1,8,8,128]{4,3,2,1,0:T(8,128)(2,1)S(1)}, u32[]{:S(2)}, u32[]{:S(2)}) collective-permute-start(bf16[3,1,8,8,128]{4,3,2,1,0:T(8,128)(2,1)S(1)} %get-tuple-element.38), channel_id=1, source_target_pairs={{0,16},{1,17},{2,18},{3,19},{4,20},{5,21},{6,22},{7,23},{8,24},{9,... | collective-permute-start | bytes 147464 | tf_op jit(solution)/shard_map/ppermute | solution.py:14
  53.9 69.6 %all_gather.6 = bf16[2048,128]{1,0:T(8,128)(2,1)S(1)} all-gather(bf16[64,128]{1,0:T(8,128)(2,1)S(1)} %convolution_convert_fusion.5), channel_id=1, replica_groups=mesh['gx'=2,'gy'=4,'gz'=4] {'gx','gy','gz'}, dimensions={0}, use_global_device_ids=true | all-gather | bytes 540672 | tf_op jit(solution)/shard_map/all_gather | solution.py:87
  125.2 3.0 collective-permute-start.2
  130.7 4.6 %collective-permute-start.4 = (bf16[3,10,10,1,128]{4,3,2,1,0:T(2,128)(2,1)S(1)}, bf16[3,10,10,1,128]{4,3,2,1,0:T(2,128)(2,1)S(1)}, u32[]{:S(2)}, u32[]{:S(2)}) collective-permute-start(bf16[3,10,10,1,128]{4,3,2,1,0:T(2,128)(2,1)S(1)} %get-tuple-element.22), channel_id=1, source_target_pairs={{0,1},{1,2},{2,3},{4,5},{5,6},{6,7},{8,9},{9,10},{10,11},{12,13},{... | collective-permute-start | bytes 230408 | tf_op jit(solution)/shard_map/ppermute | solution.py:14
  135.3 3.5 collective-permute-done.4
  140.5 9.8 %fusion.8 = f32[2048,128]{0,1:T(8,128)S(1)} fusion(bf16[1,1,1,2048,2048]{4,3,2,1,0:T(8,128)(2,1)} %param.11, bf16[512,128]{1,0:T(8,128)(2,1)S(1)} %broadcast_select_fusion.1, bf16[1536,128]{1,0:T(8,128)(2,1)S(1)} %bitcast.185), kind=kOutput, calls=%fused_computation.10 | convolution fusion | flops 2148794368 | bytes 9961472 | tf_op jit(solution)/shard_map/dot_general | solution.py:77
  155.4 4.4 %collective-permute-done.7 = bf16[3,1,8,8,128]{4,3,2,1,0:T(8,128)(2,1)S(1)} collective-permute-done((bf16[3,1,8,8,128]{4,3,2,1,0:T(8,128)(2,1)S(1)}, bf16[3,1,8,8,128]{4,3,2,1,0:T(8,128)(2,1)S(1)}, u32[]{:S(2)}, u32[]{:S(2)}) %collective-permute-start.7) | collective-permute-done | bytes 49184 | tf_op jit(solution)/shard_map/ppermute | solution.py:17
  162.4 3.9 collective-permute-done.9
  166.5 4.4 %collective-permute-start.10 = (bf16[3,10,10,1,128]{4,3,2,1,0:T(2,128)(2,1)S(1)}, bf16[3,10,10,1,128]{4,3,2,1,0:T(2,128)(2,1)S(1)}, u32[]{:S(2)}, u32[]{:S(2)}) collective-permute-start(bf16[3,10,10,1,128]{4,3,2,1,0:T(2,128)(2,1)S(1)} %get-tuple-element.19), channel_id=1, source_target_pairs={{0,1},{1,2},{2,3},{4,5},{5,6},{6,7},{8,9},{9,10},{10,11},{12,13},{... | collective-permute-start | bytes 230408 | tf_op jit(solution)/shard_map/ppermute | solution.py:14
  173.6 4.4 %collective-permute-done.11 = bf16[3,10,10,1,128]{4,3,2,1,0:T(2,128)(2,1)S(1)} collective-permute-done((bf16[3,10,10,1,128]{4,3,2,1,0:T(2,128)(2,1)S(1)}, bf16[3,10,10,1,128]{4,3,2,1,0:T(2,128)(2,1)S(1)}, u32[]{:S(2)}, u32[]{:S(2)}) %collective-permute-start.11) | collective-permute-done | bytes 76832 | tf_op jit(solution)/shard_map/ppermute | solution.py:17
  179.5 38.6 %psum.22 = f32[2,128]{1,0:T(2,128)S(1)} all-reduce(f32[2,128]{1,0:T(2,128)S(1)} %pad_maximum_fusion.33), channel_id=1, replica_groups=mesh['gx'=2,'gy'=4,'gz'=4] {'gx','gy','gz'}, use_global_device_ids=true, to_apply=%region_4.6 | all-reduce | flops 256 | bytes 2048 | tf_op jit(solution)/shard_map/psum | solution.py:46
  219.9 4.5 %collective-permute-start.12 = (bf16[3,1,8,8,128]{4,3,2,1,0:T(8,128)(2,1)S(1)}, bf16[3,1,8,8,128]{4,3,2,1,0:T(8,128)(2,1)S(1)}, u32[]{:S(2)}, u32[]{:S(2)}) collective-permute-start(bf16[3,1,8,8,128]{4,3,2,1,0:T(8,128)(2,1)S(1)} %get-tuple-element.34), channel_id=1, source_target_pairs={{0,16},{1,17},{2,18},{3,19},{4,20},{5,21},{6,22},{7,23},{8,24},{9,... | collective-permute-start | bytes 147464 | tf_op jit(solution)/shard_map/ppermute | solution.py:14
  224.5 69.6 %all_gather.7 = bf16[2048,128]{1,0:T(8,128)(2,1)S(1)} all-gather(bf16[64,128]{1,0:T(8,128)(2,1)S(1)} %convolution_convert_fusion.3), channel_id=1, replica_groups=mesh['gx'=2,'gy'=4,'gz'=4] {'gx','gy','gz'}, dimensions={0}, use_global_device_ids=true | all-gather | bytes 540672 | tf_op jit(solution)/shard_map/all_gather | solution.py:87
  295.9 3.0 collective-permute-start.14
  301.3 4.7 %collective-permute-start.16 = (bf16[3,10,10,1,128]{4,3,2,1,0:T(2,128)(2,1)S(1)}, bf16[3,10,10,1,128]{4,3,2,1,0:T(2,128)(2,1)S(1)}, u32[]{:S(2)}, u32[]{:S(2)}) collective-permute-start(bf16[3,10,10,1,128]{4,3,2,1,0:T(2,128)(2,1)S(1)} %get-tuple-element.18), channel_id=1, source_target_pairs={{0,1},{1,2},{2,3},{4,5},{5,6},{6,7},{8,9},{9,10},{10,11},{12,13},{... | collective-permute-start | bytes 230408 | tf_op jit(solution)/shard_map/ppermute | solution.py:14
  306.1 3.3 collective-permute-done.16
  312.6 10.8 %fusion.11 = f32[2048,128]{0,1:T(8,128)} fusion(bf16[1,1,1,2048,2048]{4,3,2,1,0:T(8,128)(2,1)} %param.11, bf16[512,128]{1,0:T(8,128)(2,1)S(1)} %broadcast_select_fusion, bf16[1536,128]{1,0:T(8,128)(2,1)S(1)} %bitcast.187), kind=kOutput, calls=%fused_computation.11 | convolution fusion | flops 2148794368 | bytes 9961472 | tf_op jit(solution)/shard_map/dot_general | solution.py:77
  327.2 3.3 collective-permute-start.18
  332.3 4.4 %collective-permute-done.19 = bf16[3,1,8,8,128]{4,3,2,1,0:T(8,128)(2,1)S(1)} collective-permute-done((bf16[3,1,8,8,128]{4,3,2,1,0:T(8,128)(2,1)S(1)}, bf16[3,1,8,8,128]{4,3,2,1,0:T(8,128)(2,1)S(1)}, u32[]{:S(2)}, u32[]{:S(2)}) %collective-permute-start.19) | collective-permute-done | bytes 49184 | tf_op jit(solution)/shard_map/ppermute | solution.py:17
  339.3 3.9 collective-permute-done.21
  343.4 4.4 %collective-permute-start.22 = (bf16[3,10,10,1,128]{4,3,2,1,0:T(2,128)(2,1)S(1)}, bf16[3,10,10,1,128]{4,3,2,1,0:T(2,128)(2,1)S(1)}, u32[]{:S(2)}, u32[]{:S(2)}) collective-permute-start(bf16[3,10,10,1,128]{4,3,2,1,0:T(2,128)(2,1)S(1)} %get-tuple-element.15), channel_id=1, source_target_pairs={{0,1},{1,2},{2,3},{4,5},{5,6},{6,7},{8,9},{9,10},{10,11},{12,13},{... | collective-permute-start | bytes 230408 | tf_op jit(solution)/shard_map/ppermute | solution.py:14
  350.5 4.4 %collective-permute-done.23 = bf16[3,10,10,1,128]{4,3,2,1,0:T(2,128)(2,1)S(1)} collective-permute-done((bf16[3,10,10,1,128]{4,3,2,1,0:T(2,128)(2,1)S(1)}, bf16[3,10,10,1,128]{4,3,2,1,0:T(2,128)(2,1)S(1)}, u32[]{:S(2)}, u32[]{:S(2)}) %collective-permute-start.23) | collective-permute-done | bytes 76832 | tf_op jit(solution)/shard_map/ppermute | solution.py:17
  356.5 38.6 %psum.23 = f32[3,128]{1,0:T(4,128)S(1)} all-reduce(f32[3,128]{1,0:T(4,128)S(1)} %pad_maximum_fusion.32), channel_id=1, replica_groups=mesh['gx'=2,'gy'=4,'gz'=4] {'gx','gy','gz'}, use_global_device_ids=true, to_apply=%region_8.10 | all-reduce | flops 384 | bytes 3072 | tf_op jit(solution)/shard_map/psum | solution.py:46
  (110 shorter events, 47.6 us)
Async XLA Ops:
  45.3 78.5 %collective-permute-start.1 = (bf16[3,1,8,8,128]{4,3,2,1,0:T(8,128)(2,1)S(1)}, bf16[3,1,8,8,128]{4,3,2,1,0:T(8,128)(2,1)S(1)}, u32[]{:S(2)}, u32[]{:S(2)}) collective-permute-start(bf16[3,1,8,8,128]{4,3,2,1,0:T(8,128)(2,1)S(1)} %get-tuple-element.37), channel_id=1, source_target_pairs={{16,0},{17,1},{18,2},{19,3},{20,4},{21,5},{22,6},{23,7},{24,8},{25... | collective-permute-start | bytes 147464 | tf_op jit(solution)/shard_map/ppermute | solution.py:17
  46.6 77.2 %collective-permute-start = (bf16[3,1,8,8,128]{4,3,2,1,0:T(8,128)(2,1)S(1)}, bf16[3,1,8,8,128]{4,3,2,1,0:T(8,128)(2,1)S(1)}, u32[]{:S(2)}, u32[]{:S(2)}) collective-permute-start(bf16[3,1,8,8,128]{4,3,2,1,0:T(8,128)(2,1)S(1)} %get-tuple-element.38), channel_id=1, source_target_pairs={{0,16},{1,17},{2,18},{3,19},{4,20},{5,21},{6,22},{7,23},{8,24},{9,... | collective-permute-start | bytes 147464 | tf_op jit(solution)/shard_map/ppermute | solution.py:14
  123.9 4.4 %collective-permute-start.3 = (bf16[3,10,1,8,128]{4,3,2,1,0:T(8,128)(2,1)S(1)}, bf16[3,10,1,8,128]{4,3,2,1,0:T(8,128)(2,1)S(1)}, u32[]{:S(2)}, u32[]{:S(2)}) collective-permute-start(bf16[3,10,1,8,128]{4,3,2,1,0:T(8,128)(2,1)S(1)} %get-tuple-element.29), channel_id=1, source_target_pairs={{4,0},{8,4},{12,8},{5,1},{9,5},{13,9},{6,2},{10,6},{14,10},{7,3},{... | collective-permute-start | bytes 184328 | tf_op jit(solution)/shard_map/ppermute | solution.py:17
  125.2 3.9 collective-permute-start.2
  129.4 9.5 %collective-permute-start.5 = (bf16[3,10,10,1,128]{4,3,2,1,0:T(2,128)(2,1)S(1)}, bf16[3,10,10,1,128]{4,3,2,1,0:T(2,128)(2,1)S(1)}, u32[]{:S(2)}, u32[]{:S(2)}) collective-permute-start(bf16[3,10,10,1,128]{4,3,2,1,0:T(2,128)(2,1)S(1)} %get-tuple-element.21), channel_id=1, source_target_pairs={{1,0},{2,1},{3,2},{5,4},{6,5},{7,6},{9,8},{10,9},{11,10},{13,12},{... | collective-permute-start | bytes 230408 | tf_op jit(solution)/shard_map/ppermute | solution.py:17
  130.7 8.1 %collective-permute-start.4 = (bf16[3,10,10,1,128]{4,3,2,1,0:T(2,128)(2,1)S(1)}, bf16[3,10,10,1,128]{4,3,2,1,0:T(2,128)(2,1)S(1)}, u32[]{:S(2)}, u32[]{:S(2)}) collective-permute-start(bf16[3,10,10,1,128]{4,3,2,1,0:T(2,128)(2,1)S(1)} %get-tuple-element.22), channel_id=1, source_target_pairs={{0,1},{1,2},{2,3},{4,5},{5,6},{6,7},{8,9},{9,10},{10,11},{12,13},{... | collective-permute-start | bytes 230408 | tf_op jit(solution)/shard_map/ppermute | solution.py:14
  151.0 4.4 %collective-permute-start.6 = (bf16[3,1,8,8,128]{4,3,2,1,0:T(8,128)(2,1)S(1)}, bf16[3,1,8,8,128]{4,3,2,1,0:T(8,128)(2,1)S(1)}, u32[]{:S(2)}, u32[]{:S(2)}) collective-permute-start(bf16[3,1,8,8,128]{4,3,2,1,0:T(8,128)(2,1)S(1)} %get-tuple-element.35), channel_id=1, source_target_pairs={{0,16},{1,17},{2,18},{3,19},{4,20},{5,21},{6,22},{7,23},{8,24},{9,... | collective-permute-start | bytes 147464 | tf_op jit(solution)/shard_map/ppermute | solution.py:14
  153.7 6.1 %collective-permute-start.7 = (bf16[3,1,8,8,128]{4,3,2,1,0:T(8,128)(2,1)S(1)}, bf16[3,1,8,8,128]{4,3,2,1,0:T(8,128)(2,1)S(1)}, u32[]{:S(2)}, u32[]{:S(2)}) collective-permute-start(bf16[3,1,8,8,128]{4,3,2,1,0:T(8,128)(2,1)S(1)} %get-tuple-element.36), channel_id=1, source_target_pairs={{16,0},{17,1},{18,2},{19,3},{20,4},{21,5},{22,6},{23,7},{24,8},{25... | collective-permute-start | bytes 147464 | tf_op jit(solution)/shard_map/ppermute | solution.py:17
  159.8 2.6 collective-permute-start.8
  161.1 5.2 %collective-permute-start.9 = (bf16[3,10,1,8,128]{4,3,2,1,0:T(8,128)(2,1)S(1)}, bf16[3,10,1,8,128]{4,3,2,1,0:T(8,128)(2,1)S(1)}, u32[]{:S(2)}, u32[]{:S(2)}) collective-permute-start(bf16[3,10,1,8,128]{4,3,2,1,0:T(8,128)(2,1)S(1)} %get-tuple-element.28), channel_id=1, source_target_pairs={{4,0},{8,4},{12,8},{5,1},{9,5},{13,9},{6,2},{10,6},{14,10},{7,3},{... | collective-permute-start | bytes 184328 | tf_op jit(solution)/shard_map/ppermute | solution.py:17
  166.5 7.1 %collective-permute-start.10 = (bf16[3,10,10,1,128]{4,3,2,1,0:T(2,128)(2,1)S(1)}, bf16[3,10,10,1,128]{4,3,2,1,0:T(2,128)(2,1)S(1)}, u32[]{:S(2)}, u32[]{:S(2)}) collective-permute-start(bf16[3,10,10,1,128]{4,3,2,1,0:T(2,128)(2,1)S(1)} %get-tuple-element.19), channel_id=1, source_target_pairs={{0,1},{1,2},{2,3},{4,5},{5,6},{6,7},{8,9},{9,10},{10,11},{12,13},{... | collective-permute-start | bytes 230408 | tf_op jit(solution)/shard_map/ppermute | solution.py:14
  170.9 7.1 %collective-permute-start.11 = (bf16[3,10,10,1,128]{4,3,2,1,0:T(2,128)(2,1)S(1)}, bf16[3,10,10,1,128]{4,3,2,1,0:T(2,128)(2,1)S(1)}, u32[]{:S(2)}, u32[]{:S(2)}) collective-permute-start(bf16[3,10,10,1,128]{4,3,2,1,0:T(2,128)(2,1)S(1)} %get-tuple-element.20), channel_id=1, source_target_pairs={{1,0},{2,1},{3,2},{5,4},{6,5},{7,6},{9,8},{10,9},{11,10},{13,12},{... | collective-permute-start | bytes 230408 | tf_op jit(solution)/shard_map/ppermute | solution.py:17
  218.6 75.9 %collective-permute-start.13 = (bf16[3,1,8,8,128]{4,3,2,1,0:T(8,128)(2,1)S(1)}, bf16[3,1,8,8,128]{4,3,2,1,0:T(8,128)(2,1)S(1)}, u32[]{:S(2)}, u32[]{:S(2)}) collective-permute-start(bf16[3,1,8,8,128]{4,3,2,1,0:T(8,128)(2,1)S(1)} %get-tuple-element.33), channel_id=1, source_target_pairs={{16,0},{17,1},{18,2},{19,3},{20,4},{21,5},{22,6},{23,7},{24,8},{25... | collective-permute-start | bytes 147464 | tf_op jit(solution)/shard_map/ppermute | solution.py:17
  219.9 74.6 %collective-permute-start.12 = (bf16[3,1,8,8,128]{4,3,2,1,0:T(8,128)(2,1)S(1)}, bf16[3,1,8,8,128]{4,3,2,1,0:T(8,128)(2,1)S(1)}, u32[]{:S(2)}, u32[]{:S(2)}) collective-permute-start(bf16[3,1,8,8,128]{4,3,2,1,0:T(8,128)(2,1)S(1)} %get-tuple-element.34), channel_id=1, source_target_pairs={{0,16},{1,17},{2,18},{3,19},{4,20},{5,21},{6,22},{7,23},{8,24},{9,... | collective-permute-start | bytes 147464 | tf_op jit(solution)/shard_map/ppermute | solution.py:14
  294.6 4.4 %collective-permute-start.15 = (bf16[3,10,1,8,128]{4,3,2,1,0:T(8,128)(2,1)S(1)}, bf16[3,10,1,8,128]{4,3,2,1,0:T(8,128)(2,1)S(1)}, u32[]{:S(2)}, u32[]{:S(2)}) collective-permute-start(bf16[3,10,1,8,128]{4,3,2,1,0:T(8,128)(2,1)S(1)} %get-tuple-element.25), channel_id=1, source_target_pairs={{4,0},{8,4},{12,8},{5,1},{9,5},{13,9},{6,2},{10,6},{14,10},{7,3},{... | collective-permute-start | bytes 184328 | tf_op jit(solution)/shard_map/ppermute | solution.py:17
  295.9 3.9 collective-permute-start.14
  300.0 9.5 %collective-permute-start.17 = (bf16[3,10,10,1,128]{4,3,2,1,0:T(2,128)(2,1)S(1)}, bf16[3,10,10,1,128]{4,3,2,1,0:T(2,128)(2,1)S(1)}, u32[]{:S(2)}, u32[]{:S(2)}) collective-permute-start(bf16[3,10,10,1,128]{4,3,2,1,0:T(2,128)(2,1)S(1)} %get-tuple-element.17), channel_id=1, source_target_pairs={{1,0},{2,1},{3,2},{5,4},{6,5},{7,6},{9,8},{10,9},{11,10},{13,12},{... | collective-permute-start | bytes 230408 | tf_op jit(solution)/shard_map/ppermute | solution.py:17
  301.3 8.1 %collective-permute-start.16 = (bf16[3,10,10,1,128]{4,3,2,1,0:T(2,128)(2,1)S(1)}, bf16[3,10,10,1,128]{4,3,2,1,0:T(2,128)(2,1)S(1)}, u32[]{:S(2)}, u32[]{:S(2)}) collective-permute-start(bf16[3,10,10,1,128]{4,3,2,1,0:T(2,128)(2,1)S(1)} %get-tuple-element.18), channel_id=1, source_target_pairs={{0,1},{1,2},{2,3},{4,5},{5,6},{6,7},{8,9},{9,10},{10,11},{12,13},{... | collective-permute-start | bytes 230408 | tf_op jit(solution)/shard_map/ppermute | solution.py:14
  327.2 5.1 %collective-permute-start.18 = (bf16[3,1,8,8,128]{4,3,2,1,0:T(8,128)(2,1)S(1)}, bf16[3,1,8,8,128]{4,3,2,1,0:T(8,128)(2,1)S(1)}, u32[]{:S(2)}, u32[]{:S(2)}) collective-permute-start(bf16[3,1,8,8,128]{4,3,2,1,0:T(8,128)(2,1)S(1)} %get-tuple-element.31), channel_id=1, source_target_pairs={{0,16},{1,17},{2,18},{3,19},{4,20},{5,21},{6,22},{7,23},{8,24},{9,... | collective-permute-start | bytes 147464 | tf_op jit(solution)/shard_map/ppermute | solution.py:14
  330.6 6.1 %collective-permute-start.19 = (bf16[3,1,8,8,128]{4,3,2,1,0:T(8,128)(2,1)S(1)}, bf16[3,1,8,8,128]{4,3,2,1,0:T(8,128)(2,1)S(1)}, u32[]{:S(2)}, u32[]{:S(2)}) collective-permute-start(bf16[3,1,8,8,128]{4,3,2,1,0:T(8,128)(2,1)S(1)} %get-tuple-element.32), channel_id=1, source_target_pairs={{16,0},{17,1},{18,2},{19,3},{20,4},{21,5},{22,6},{23,7},{24,8},{25... | collective-permute-start | bytes 147464 | tf_op jit(solution)/shard_map/ppermute | solution.py:17
  336.7 2.6 collective-permute-start.20
  338.0 5.2 %collective-permute-start.21 = (bf16[3,10,1,8,128]{4,3,2,1,0:T(8,128)(2,1)S(1)}, bf16[3,10,1,8,128]{4,3,2,1,0:T(8,128)(2,1)S(1)}, u32[]{:S(2)}, u32[]{:S(2)}) collective-permute-start(bf16[3,10,1,8,128]{4,3,2,1,0:T(8,128)(2,1)S(1)} %get-tuple-element.24), channel_id=1, source_target_pairs={{4,0},{8,4},{12,8},{5,1},{9,5},{13,9},{6,2},{10,6},{14,10},{7,3},{... | collective-permute-start | bytes 184328 | tf_op jit(solution)/shard_map/ppermute | solution.py:17
  343.4 7.1 %collective-permute-start.22 = (bf16[3,10,10,1,128]{4,3,2,1,0:T(2,128)(2,1)S(1)}, bf16[3,10,10,1,128]{4,3,2,1,0:T(2,128)(2,1)S(1)}, u32[]{:S(2)}, u32[]{:S(2)}) collective-permute-start(bf16[3,10,10,1,128]{4,3,2,1,0:T(2,128)(2,1)S(1)} %get-tuple-element.15), channel_id=1, source_target_pairs={{0,1},{1,2},{2,3},{4,5},{5,6},{6,7},{8,9},{9,10},{10,11},{12,13},{... | collective-permute-start | bytes 230408 | tf_op jit(solution)/shard_map/ppermute | solution.py:14
  347.8 7.1 %collective-permute-start.23 = (bf16[3,10,10,1,128]{4,3,2,1,0:T(2,128)(2,1)S(1)}, bf16[3,10,10,1,128]{4,3,2,1,0:T(2,128)(2,1)S(1)}, u32[]{:S(2)}, u32[]{:S(2)}) collective-permute-start(bf16[3,10,10,1,128]{4,3,2,1,0:T(2,128)(2,1)S(1)} %get-tuple-element.16), channel_id=1, source_target_pairs={{1,0},{2,1},{3,2},{5,4},{6,5},{7,6},{9,8},{10,9},{11,10},{13,12},{... | collective-permute-start | bytes 230408 | tf_op jit(solution)/shard_map/ppermute | solution.py:17
  (7 other events, 264.5 us)
where the time goes:
time: 398 us; the launch traced here: 397 us
  blocking collectives  258 us (65%)
  starting transfers between devices  57.5 us (14%)
  waiting for transfers between devices  37.2 us (9%)
  matrix products  25.7 us (6%)
  other arithmetic  11 us (3%)
  local copies, waits for them, and re-layouts  5.55 us (1%)
    all_gather x2, blocking collectives, precondition(): lax.all_gather(placed, ('gx', 'gy', 'gz'), axis=0, tiled=True)  139 us
    psum x2, blocking collectives, orthogonalize(): totals = lax.psum(partials, ('gx', 'gy', 'gz'))  77.2 us
    psum x1, blocking collectives, norm_sum(): return lax.psum(inner(field, field), ('gx', 'gy', 'gz'))  42 us
    ppermute x12, starting transfers between devices, with_halo(): lax.ppermute(lax.slice_in_dim(block, block.shape[dim] - width, None, axis...  41.8 us
    ppermute x12, waiting for transfers between devices, with_halo(): lax.ppermute(lax.slice_in_dim(block, 0, width, axis=dim), axis, backward)  25.4 us
    dot_general x2, matrix products, precondition(): lax.dot_general(factor, front_values, contract_first, preferred_element_t...  20.7 us
    ppermute x12, starting transfers between devices, with_halo(): lax.ppermute(lax.slice_in_dim(block, 0, width, axis=dim), axis, backward)  15.8 us
    ppermute x12, waiting for transfers between devices, with_halo(): lax.ppermute(lax.slice_in_dim(block, block.shape[dim] - width, None, axis...  11.8 us
  transfers between devices with their start and end apart: 24, of which 14 were waited for; matrix products, arithmetic and copies ran while one was open for 1% of the time, Pallas kernels for 0%

commit v1 on v0

v1 whole, which is shorter than its diff:
```python
import functools
import jax
import jax.numpy as jnp
from jax import lax
from jax.experimental import pallas as pl
from jax.experimental.pallas import tpu as pltpu
from jax.sharding import PartitionSpec as P

EPSILON = 1e-06
AXES = ("gx", "gy", "gz")
MESH = pl.DeviceIdType.MESH
F32 = jnp.float32
BF16 = jnp.bfloat16


def dot(a, b):
    return jnp.dot(a, b, preferred_element_type=F32)


def kernel(
    dims,
    cells,
    right_hbm,
    stiff_ref,
    factor_hbm,
    basis_hbm,
    map_ref,
    margin_ref,
    inverse_hbm,
    solution_ref,
    ratio_ref,
    right,
    factor,
    basis,
    inverse,
    own,
    placed_basis,
    onehot,
    face_factor,
    diagonal,
    search,
    image,
    zpad,
    front,
    back,
    send_faces,
    faces,
    coarse,
    sums_z,
    sums_xy,
    load_sem,
    factor_sem,
    face_send,
    face_recv,
    coarse_send,
    coarse_recv,
    sum_send,
    sum_recv,
):
    count_x, count_y, count_z = dims
    comps, cx, cy, cz = cells
    plane = cy * cz
    slab = cx * plane
    rows = comps * slab
    size = factor.shape[0]
    blk = 256
    own_blocks, all_blocks = rows // blk, size // blk
    gx, gy, gz = (lax.axis_index(axis) for axis in AXES)
    low_count = coarse.shape[3]
    high_count = count_y // low_count
    gy_high, gy_low = lax.div(gy, low_count), lax.rem(gy, low_count)
    plane_id = gx * count_y + gy

    loads = [
        pltpu.make_async_copy(src, dst, load_sem.at[i])
        for i, (src, dst) in enumerate(
            [(right_hbm, right), (basis_hbm, basis), (inverse_hbm, inverse)]
        )
    ]
    loads[0].start()
    loads[1].start()
    factor_loads = []
    for i in range(all_blocks):
        part = (pl.ds(i * blk, blk), pl.ds(0, (i + 1) * blk))
        factor_loads.append(
            pltpu.make_async_copy(factor_hbm.at[part], factor.at[part], factor_sem.at[i])
        )
        factor_loads[-1].start()
    loads[2].start()

    barrier = pltpu.get_barrier_semaphore()
    z_peers = [{"gz": lax.rem(gz + d, count_z)} for d in range(1, count_z)]
    xy_peers = []
    for d in range(1, count_x * count_y):
        other = lax.rem(plane_id + d, count_x * count_y)
        xy_peers.append({"gx": lax.div(other, count_y), "gy": lax.rem(other, count_y)})
    for peer in z_peers + xy_peers:
        pl.semaphore_signal(barrier, inc=1, device_id=peer, device_id_type=MESH)

    here = (gx, gx, gy, gy, gz, gz)
    counts = (count_x, count_x, count_y, count_y, count_z, count_z)
    present = [
        here[f] > 0 if f % 2 == 0 else here[f] < counts[f] - 1 for f in range(6)
    ]
    for f in range(6):

        @pl.when(jnp.logical_not(present[f]))
        def _():
            for e in range(4):
                faces[e, f] = jnp.zeros(faces.shape[2:], BF16)

    eye = lax.broadcasted_iota(jnp.int32, (cz, cz), 0) == lax.broadcasted_iota(
        jnp.int32, (cz, cz), 1
    )

    def fill(i, carry):
        tile = stiff_ref[i]
        for y in range(cy):
            line = jnp.sum(jnp.where(eye, tile[y : y + 1, :], 0.0), axis=1, keepdims=True)
            start = pl.multiple_of(i * plane + y * cz, cz)
            diagonal[pl.ds(start, cz), :] = jnp.broadcast_to(line + 6.0, (cz, right.shape[1]))
        return carry

    lax.fori_loop(0, comps * cx, fill, 0)

    margin = margin_ref[...]
    for f in range(6):
        for c in range(comps):
            ids = lax.broadcasted_iota(jnp.int32, (plane, margin.shape[1]), 0) + (
                (c * 6 + f) * plane
            )
            onehot[pl.ds((f * comps + c) * plane, plane), :] = jnp.where(
                ids == margin, 1.0, 0.0
            ).astype(BF16)

    def face_copy(e, f):
        step = 1 if f % 2 else -1
        axis = AXES[f // 2]
        return pltpu.make_async_remote_copy(
            src_ref=send_faces.at[e, f],
            dst_ref=faces.at[e, f ^ 1],
            send_sem=face_send.at[e, f],
            recv_sem=face_recv.at[e, f ^ 1],
            device_id={axis: here[f] + step},
            device_id_type=MESH,
        )

    def face_arrival(e, f):
        return pltpu.make_async_remote_copy(
            src_ref=send_faces.at[e, f],
            dst_ref=faces.at[e, f],
            send_sem=face_send.at[e, f],
            recv_sem=face_recv.at[e, f],
            device_id={AXES[f // 2]: here[f]},
            device_id_type=MESH,
        )

    def pack_faces(e, field):
        for f in range(6):
            for c in range(comps):
                base = c * slab
                if f < 2:
                    x = 0 if f == 0 else cx - 1
                    piece = field[pl.ds(base + x * plane, plane), :]
                elif f < 4:
                    y = 0 if f == 2 else cy - 1
                    piece = jnp.concatenate(
                        [field[pl.ds(base + x * plane + y * cz, cz), :] for x in range(cx)], axis=0
                    )
                else:
                    z = 0 if f == 4 else cz - 1
                    piece = field[pl.ds(base + z, cx * cy, stride=cz), :]
                send_faces[e, f, pl.ds(c * plane, plane), :] = piece.astype(BF16)

            @pl.when(present[f])
            def _():
                face_copy(e, f).start()

    def wait_faces(e):
        for f in range(6):

            @pl.when(present[f])
            def _():
                face_arrival(e, f).wait_recv()

    def coarse_stages(k):
        def copy(view, peer, number):
            return pltpu.make_async_remote_copy(
                src_ref=view,
                dst_ref=view,
                send_sem=coarse_send.at[k, number],
                recv_sem=coarse_recv.at[k, number],
                device_id=peer,
                device_id_type=MESH,
            )

        stages, number = [], 0
        plan = [
            (coarse.at[k, gx, gy_high, gy_low, gz], count_z, lambda d: {"gz": lax.rem(gz + d, count_z)}),
            (coarse.at[k, gx, gy_high, gy_low], count_x, lambda d: {"gx": lax.rem(gx + d, count_x)}),
            (
                coarse.at[k, :, gy_high, gy_low],
                high_count,
                lambda d: {"gy": lax.rem(gy_high + d, high_count) * low_count + gy_low},
            ),
            (
                coarse.at[k, :, :, gy_low],
                low_count,
                lambda d: {"gy": gy_high * low_count + lax.rem(gy_low + d, low_count)},
            ),
        ]
        for view, count, peer in plan:
            stage = []
            for d in range(1, count):
                stage.append(copy(view, peer(d), number))
                number += 1
            stages.append(stage)
        return stages

    def start(stage):
        for copy in stage:
            copy.start()

    def arrive(stage):
        for copy in stage:
            copy.wait_recv()

    every_stage = []

    def precondition(k, e):
        residual = dot(placed_basis[...], own[...]).astype(BF16)
        coarse[k, gx, gy_high, gy_low, gz] = residual
        stages = coarse_stages(k)
        every_stage.extend(stages)
        start(stages[0])
        for i in range(own_blocks):
            if k == 0:
                factor_loads[i].wait()
            values = dot(factor[pl.ds(i * blk, blk), pl.ds(0, (i + 1) * blk)], own[pl.ds(0, (i + 1) * blk), :])
            front[:, pl.ds(i * blk, blk)] = values.T.astype(BF16)
        arrive(stages[0])
        start(stages[1])
        for j in range(own_blocks):
            back[:, pl.ds(j * blk, blk)] = dot(
                front[:, pl.ds(j * blk, rows - j * blk)],
                factor[pl.ds(j * blk, rows - j * blk), pl.ds(j * blk, blk)],
            )
        arrive(stages[1])
        start(stages[2])
        if k == 0:
            for i in range(own_blocks, all_blocks):
                factor_loads[i].wait()
                wide = (i + 1) * blk - rows
                face_factor[pl.ds(i * blk - rows, blk), :] = lax.dot_general(
                    factor[pl.ds(i * blk, blk), pl.ds(rows, wide)],
                    onehot[:, pl.ds(0, wide)],
                    (((1,), (1,)), ((), ())),
                    preferred_element_type=F32,
                ).astype(BF16)
        wait_faces(e)
        margin_faces = faces[e].reshape(-1, faces.shape[-1])
        for i in range(own_blocks, all_blocks):
            values = dot(factor[pl.ds(i * blk, blk), pl.ds(0, rows)], own[...]) + dot(
                face_factor[pl.ds(i * blk - rows, blk), :], margin_faces
            )
            front[:, pl.ds(i * blk, blk)] = values.T.astype(BF16)
        arrive(stages[2])
        start(stages[3])
        for j in range(own_blocks):
            back[:, pl.ds(j * blk, blk)] += dot(
                front[:, pl.ds(rows, size - rows)],
                factor[pl.ds(rows, size - rows), pl.ds(j * blk, blk)],
            )
        if k == 0:
            loads[2].wait()
        arrive(stages[3])
        solved = dot(inverse[...], coarse[k].reshape(-1, coarse.shape[-1]))
        solved = solved.T.astype(BF16)
        for j in range(own_blocks):
            cut = pl.ds(j * blk, blk)
            search[k, cut, :] = (back[:, cut] + dot(solved, placed_basis[:, cut])).T

    def operate(k, e):
        field = search.at[k]
        wait_faces(e)
        zi = lax.broadcasted_iota(jnp.int32, (cy, cz, right.shape[1]), 1)
        totals = None
        for c in range(comps):
            base = c * slab
            cut = pl.ds(c * plane, plane)
            x_low, x_high, y_low, y_high, z_low, z_high = (
                faces[e, f, cut, :].astype(F32) for f in range(6)
            )
            zpad[pl.ds(base, cx * cy, stride=cz), :] = z_low
            zpad[pl.ds(base + cz - 1, cx * cy, stride=cz), :] = z_high
            for x in range(cx):
                at = pl.ds(base + x * plane, plane)
                flat = field[at, :]
                center = flat.reshape(cy, cz, -1)
                lower = field[pl.ds(base + (x - 1) * plane, plane), :] if x else x_low
                upper = field[pl.ds(base + (x + 1) * plane, plane), :] if x < cx - 1 else x_high
                edge = zpad[at, :].reshape(cy, cz, -1)
                beside = (lower + upper).reshape(cy, cz, -1)
                beside += jnp.concatenate([y_low[x * cz : (x + 1) * cz][None], center[:-1]], axis=0)
                beside += jnp.concatenate([center[1:], y_high[x * cz : (x + 1) * cz][None]], axis=0)
                beside += jnp.where(zi == 0, edge, pltpu.roll(center, 1, axis=1))
                beside += jnp.where(zi == cz - 1, edge, pltpu.roll(center, cz - 1, axis=1))
                out = diagonal[at, :].reshape(cy, cz, -1) * center - beside
                given = right[at, :].reshape(cy, cz, -1)
                if k == 0:
                    flat_out = out.reshape(plane, -1)
                    image[at, :] = flat_out
                    own[at, :] = flat_out.astype(BF16)
                    terms = [given * given, out * given, out * out]
                else:
                    first = image[at, :].reshape(cy, cz, -1)
                    terms = [out * given, out * first, out * out]
                terms = [jnp.sum(term, axis=0) for term in terms]
                totals = terms if totals is None else [a + b for a, b in zip(totals, terms)]
        for q, total in enumerate(totals):
            sums_z[gz, pl.ds(k * 3 + q, 1), :] = jnp.sum(total, axis=0, keepdims=True)

    sums_z[gz] = jnp.zeros(sums_z.shape[1:], F32)
    loads[1].wait()
    ids = lax.broadcasted_iota(jnp.int32, (basis.shape[0], basis.shape[0]), 0)
    table = jnp.where(ids == map_ref[...], 1.0, 0.0).astype(BF16)
    placed_basis[...] = dot(table, basis[...]).astype(BF16)
    loads[0].wait()
    own[...] = right[...].astype(BF16)
    pl.semaphore_wait(barrier, len(z_peers) + len(xy_peers))
    pack_faces(0, right)
    precondition(0, 0)
    pack_faces(1, search.at[0])
    operate(0, 1)
    pack_faces(2, image)
    precondition(1, 2)
    pack_faces(3, search.at[1])
    operate(1, 3)

    sum_copies = []

    def share(slots, index, peers, base):
        copies = []
        for n, peer in enumerate(peers):
            copies.append(
                pltpu.make_async_remote_copy(
                    src_ref=slots.at[index],
                    dst_ref=slots.at[index],
                    send_sem=sum_send.at[base + n],
                    recv_sem=sum_recv.at[base + n],
                    device_id=peer,
                    device_id_type=MESH,
                )
            )
        start(copies)
        arrive(copies)
        sum_copies.extend(copies)
        total = slots[0]
        for n in range(1, slots.shape[0]):
            total = total + slots[n]
        return total

    sums_xy[plane_id] = share(sums_z, gz, z_peers, 0)
    total = share(sums_xy, plane_id, xy_peers, len(z_peers))
    vv, iv, ii, tv, ti, tt = (total[q : q + 1] for q in range(6))

    start_square = vv + EPSILON
    start_norm = jnp.sqrt(start_square)
    along_one = iv / start_square
    rest = jnp.maximum(
        ii / start_square - along_one * along_one * (2.0 - vv / start_square), 0.0
    )
    square_two = rest + EPSILON
    norm_two = jnp.sqrt(square_two)
    scale = start_norm * norm_two
    cross_two = (tv - along_one * iv) / (start_square * norm_two)
    along_two = (ti - along_one * ii - along_one * (tv - along_one * iv)) / (
        start_square * square_two
    )
    square_image = (tt - along_one * (2.0 * ti - along_one * ii)) / (start_square * square_two)
    overlap = (iv - along_one * vv) / (start_square * norm_two)
    rest = (
        square_image
        - cross_two * cross_two * (2.0 - vv / start_square)
        - along_two * along_two * (2.0 - rest / square_two)
        + 2.0 * cross_two * along_two * overlap
    )
    norm_three = jnp.sqrt(jnp.maximum(rest, 0.0) + EPSILON)
    radius_one = jnp.sqrt(along_one * along_one + square_two)
    cosine_one = along_one / radius_one
    sine_one = norm_two / radius_one
    turned_one = cosine_one * cross_two + sine_one * along_two
    turned_two = cosine_one * along_two - sine_one * cross_two
    radius_two = jnp.sqrt(turned_two * turned_two + norm_three * norm_three)
    cosine_two = turned_two / radius_two
    sine_two = norm_three / radius_two
    coef_two = -cosine_two * sine_one * start_norm / radius_two
    coef_one = (cosine_one * start_norm - turned_one * coef_two) / radius_one
    ratio_ref[...] = sine_one * sine_two
    weight_two = coef_two / scale
    weight_one = coef_one / start_norm - along_one * weight_two
    solution_ref[...] = weight_one * search[0] + weight_two * search[1]

    for stage in every_stage + [sum_copies]:
        for copy in stage:
            copy.wait_send()
    for e in range(4):
        for f in range(6):

            @pl.when(present[f])
            def _():
                face_copy(e, f).wait_send()


def local(dims, right_side, stiffness, local_factor, basis, coarse_map, margin_index, coarse_inverse):
    cells = right_side.shape[:4]
    comps, cx, cy, cz = cells
    rhs = right_side.shape[-1]
    rows = comps * cx * cy * cz
    size = local_factor.shape[-1]
    functions = basis.shape[-2]
    margin = margin_index.shape[-1]
    face = comps * cy * cz
    assert cx == cy == cz and rows % 256 == 0 and size % 256 == 0
    low_count = 2 if dims[1] % 2 == 0 else 1
    devices = dims[0] * dims[1] * dims[2]
    copies = sum(n - 1 for n in (dims[2], dims[0], dims[1] // low_count, low_count))
    sum_copies = dims[2] - 1 + dims[0] * dims[1] - 1
    anywhere = pl.BlockSpec(memory_space=pl.ANY)
    vmem = pl.BlockSpec(memory_space=pltpu.VMEM)
    solved, ratio = pl.pallas_call(
        functools.partial(kernel, dims, cells),
        out_shape=(
            jax.ShapeDtypeStruct((rows, rhs), F32),
            jax.ShapeDtypeStruct((1, rhs), F32),
        ),
        in_specs=[anywhere, vmem, anywhere, anywhere, vmem, vmem, anywhere],
        out_specs=(vmem, vmem),
        scratch_shapes=[
            pltpu.VMEM((rows, rhs), F32),
            pltpu.VMEM((size, size), BF16),
            pltpu.VMEM((functions, rows), BF16),
            pltpu.VMEM(coarse_inverse.shape, BF16),
            pltpu.VMEM((rows, rhs), BF16),
            pltpu.VMEM((functions, rows), BF16),
            pltpu.VMEM((6 * face, margin), BF16),
            pltpu.VMEM((margin, 6 * face), BF16),
            pltpu.VMEM((rows, rhs), F32),
            pltpu.VMEM((2, rows, rhs), F32),
            pltpu.VMEM((rows, rhs), F32),
            pltpu.VMEM((rows, rhs), F32),
            pltpu.VMEM((rhs, size), BF16),
            pltpu.VMEM((rhs, rows), F32),
            pltpu.VMEM((4, 6, face, rhs), BF16),
            pltpu.VMEM((4, 6, face, rhs), BF16),
            pltpu.VMEM(
                (2, dims[0], dims[1] // low_count, low_count, dims[2], functions, rhs), BF16
            ),
            pltpu.VMEM((dims[2], 8, rhs), F32),
            pltpu.VMEM((dims[0] * dims[1], 8, rhs), F32),
            pltpu.SemaphoreType.DMA((3,)),
            pltpu.SemaphoreType.DMA((size // 256,)),
            pltpu.SemaphoreType.DMA((4, 6)),
            pltpu.SemaphoreType.DMA((4, 6)),
            pltpu.SemaphoreType.DMA((2, copies)),
            pltpu.SemaphoreType.DMA((2, copies)),
            pltpu.SemaphoreType.DMA((sum_copies,)),
            pltpu.SemaphoreType.DMA((sum_copies,)),
        ],
        compiler_params=pltpu.CompilerParams(
            collective_id=0, has_side_effects=True, vmem_limit_bytes=56 * 1024 * 1024
        ),
    )(
        right_side.reshape(rows, rhs),
        stiffness.reshape(comps * cx, cy, cz),
        local_factor.reshape(size, size),
        basis.reshape(functions, rows),
        coarse_map.reshape(1, functions),
        margin_index.reshape(1, margin),
        coarse_inverse,
    )
    return solved.reshape(right_side.shape), ratio.reshape(rhs)


def solution(mesh):
    dims = tuple(mesh.shape[axis] for axis in AXES)
    return jax.shard_map(
        functools.partial(local, dims),
        mesh=mesh,
        in_specs=(
            P(None, "gx", "gy", "gz", None),
            P(None, "gx", "gy", "gz"),
            P("gx", "gy", "gz", None, None),
            P("gx", "gy", "gz", None, None),
            P("gx", "gy", "gz", None),
            P("gx", "gy", "gz", None),
            P(("gx", "gy", "gz"), None),
        ),
        out_specs=(P(None, "gx", "gy", "gz", None), P()),
        check_vma=False,
    )
```

time: 398 us -> 54.1 us (0.14)
  blocking collectives: 258 us -> 0 us
  starting transfers between devices: 57.5 us -> 0 us
  Pallas kernels: 0 us -> 50.1 us
  waiting for transfers between devices: 37.2 us -> 0 us
  matrix products: 25.7 us -> 0 us
  other arithmetic: 11 us -> 0 us
    all_gather x2 -> x0, blocking collectives: 139 us -> none  [precondition(): lax.all_gather(placed, ('gx', 'gy', 'gz'), axis=0, tiled=True)]
    psum x3 -> x0, blocking collectives: 119 us -> none  [the longest x2 77.2 us: orthogonalize(): totals = lax.psum(partials, ('gx', 'gy', 'gz'))]
    ppermute x24 -> x0, starting transfers between devices: 57.5 us -> none  [the longest x12 41.8 us: with_halo(): lax.ppermute(lax.slice_in_dim(block, block.shape[dim] - width, None, axis...]
    pallas_call x0 -> x1, Pallas kernels: none -> 50.1 us  [local(): pl.pallas_call(functools.partial(kernel, dims, cells), out_shape=(jax.Sha...]
    ppermute x24 -> x0, waiting for transfers between devices: 37.2 us -> none  [the longest x12 25.4 us: with_halo(): lax.ppermute(lax.slice_in_dim(block, 0, width, axis=dim), axis, backward)]
    dot_general x12 -> x0, matrix products: 25.7 us -> none  [the longest x2 20.7 us: precondition(): lax.dot_general(factor, front_values, contract_first, preferred_element_t...]
  transfers between devices with their start and end apart: 24 -> 0, of which waited for: 14 -> 0; matrix products, arithmetic and copies ran while one was open for 1% -> 0% of each run, Pallas kernels for 0% -> 0%
where the time goes in v1:
time: 54.1 us; the launch traced here: 53.9 us
  Pallas kernels  50.1 us (93%)
  local copies, waits for them, and re-layouts  3.17 us (6%)
  between operations  0.64 us (1%)
    pallas_call x1, Pallas kernels, local(): pl.pallas_call(functools.partial(kernel, dims, cells), out_shape=(jax.Sha...  50.1 us
    unnamed x2, local copies, waits for them, and re-layouts  3.17 us

profile of v1, /device:TPU:0, one launch (start us, length us, event | category | flops | bytes accessed | tf_op | source)
XLA Modules:
  0.0 53.9 jit_solution(10450299555870332609)
XLA Ops:
  0.6 50.1 %shard_map.86 = (f32[1536,128]{1,0:T(8,128)}, f32[1,128]{1,0:T(1,128)}) custom-call(f32[1536,128]{1,0:T(8,128)} %bitcast.10, f32[24,8,8]{2,1,0:T(8,128)} %bitcast.12, bf16[2048,2048]{1,0:T(8,128)(2,1)} %bitcast.8, bf16[64,1536]{1,0:T(8,128)(2,1)} %bitcast.11, s32[1,64]{1,0:T(1,128)} %bitcast.14, s32[1,512]{1,0:T(1,128)} %bitcast.13, bf16[64,2048]{1,0:T(8,128)(2,1)} %inverse_hbm.1), custom_call_target="tpu_custom_call" | custom-call | tf_op jit(solution)/shard_map/pallas_call | solution.py:431
  50.7 2.1 %copy.11 = f32[3,8,8,8,128]{4,3,2,1,0:T(8,128)} copy(f32[3,8,8,8,128]{4,3,2,1,0:T(8,128)} %bitcast.9) | data formatting | bytes 1572864
  52.8 1.1 %copy.12 = f32[128]{0:T(128)} copy(f32[128]{0:T(128)} %bitcast.15) | data formatting | bytes 1024

commit v2 on v1

--- a/solution.py
+++ b/solution.py
@@ -27,20 +27,21 @@
     map_ref,
     margin_ref,
     inverse_hbm,
-    solution_ref,
-    ratio_ref,
+    search_one_hbm,
+    search_two_hbm,
+    weights_ref,
     right,
     factor,
     basis,
     inverse,
     own,
     placed_basis,
+    placed_turned,
     onehot,
     face_factor,
     diagonal,
     search,
-    image,
-    zpad,
+    images,
     front,
     back,
     send_faces,
@@ -56,6 +57,7 @@
     coarse_recv,
     sum_send,
     sum_recv,
+    out_sem,
 ):
     count_x, count_y, count_z = dims
     comps, cx, cy, cz = cells
@@ -109,30 +111,6 @@
             for e in range(4):
                 faces[e, f] = jnp.zeros(faces.shape[2:], BF16)
 
-    eye = lax.broadcasted_iota(jnp.int32, (cz, cz), 0) == lax.broadcasted_iota(
-        jnp.int32, (cz, cz), 1
-    )
-
-    def fill(i, carry):
-        tile = stiff_ref[i]
-        for y in range(cy):
-            line = jnp.sum(jnp.where(eye, tile[y : y + 1, :], 0.0), axis=1, keepdims=True)
-            start = pl.multiple_of(i * plane + y * cz, cz)
-            diagonal[pl.ds(start, cz), :] = jnp.broadcast_to(line + 6.0, (cz, right.shape[1]))
-        return carry
-
-    lax.fori_loop(0, comps * cx, fill, 0)
-
-    margin = margin_ref[...]
-    for f in range(6):
-        for c in range(comps):
-            ids = lax.broadcasted_iota(jnp.int32, (plane, margin.shape[1]), 0) + (
-                (c * 6 + f) * plane
-            )
-            onehot[pl.ds((f * comps + c) * plane, plane), :] = jnp.where(
-                ids == margin, 1.0, 0.0
-            ).astype(BF16)
-
     def face_copy(e, f):
         step = 1 if f % 2 else -1
         axis = AXES[f // 2]
@@ -196,23 +174,14 @@
 
         stages, number = [], 0
         plan = [
-            (coarse.at[k, gx, gy_high, gy_low, gz], count_z, lambda d: {"gz": lax.rem(gz + d, count_z)}),
-            (coarse.at[k, gx, gy_high, gy_low], count_x, lambda d: {"gx": lax.rem(gx + d, count_x)}),
-            (
-                coarse.at[k, :, gy_high, gy_low],
-                high_count,
-                lambda d: {"gy": lax.rem(gy_high + d, high_count) * low_count + gy_low},
-            ),
-            (
-                coarse.at[k, :, :, gy_low],
-                low_count,
-                lambda d: {"gy": gy_high * low_count + lax.rem(gy_low + d, low_count)},
-            ),
+            (coarse.at[k, gx, gy_high, gy_low, gz], z_peers),
+            (coarse.at[k, gx, gy_high, gy_low], [(lambda o: {"gx": lax.div(o, high_count), "gy": lax.rem(o, high_count) * low_count + gy_low})(lax.rem(gx * high_count + gy_high + d, count_x * high_count)) for d in range(1, count_x * high_count)]),
+            (coarse.at[k, :, :, gy_low], [{"gy": gy_high * low_count + lax.rem(gy_low + d, low_count)} for d in range(1, low_count)]),
         ]
-        for view, count, peer in plan:
+        for view, peers in plan:
             stage = []
-            for d in range(1, count):
-                stage.append(copy(view, peer(d), number))
+            for peer in peers:
+                stage.append(copy(view, peer, number))
                 number += 1
             stages.append(stage)
         return stages
@@ -227,26 +196,56 @@
 
     every_stage = []
 
-    def precondition(k, e):
+    def prepare():
+        eye = lax.broadcasted_iota(jnp.int32, (cz, cz), 0) == lax.broadcasted_iota(
+            jnp.int32, (cz, cz), 1
+        )
+
+        def fill(i, carry):
+            tile = stiff_ref[i]
+            for y in range(cy):
+                line = jnp.sum(jnp.where(eye, tile[y : y + 1, :], 0.0), axis=1, keepdims=True)
+                start = pl.multiple_of(i * plane + y * cz, cz)
+                diagonal[pl.ds(start, cz), :] = jnp.broadcast_to(line + 6.0, (cz, right.shape[1]))
+            return carry
+
+        lax.fori_loop(0, comps * cx, fill, 0)
+
+        margin = margin_ref[...]
+        for f in range(6):
+            for c in range(comps):
+                ids = lax.broadcasted_iota(jnp.int32, (plane, margin.shape[1]), 0) + (
+                    (c * 6 + f) * plane
+                )
+                onehot[pl.ds((f * comps + c) * plane, plane), :] = jnp.where(
+                    ids == margin, 1.0, 0.0
+                ).astype(BF16)
+        placed_turned[...] = placed_basis[...].astype(F32).T.astype(BF16)
+
+    def precondition(k, e, field):
         residual = dot(placed_basis[...], own[...]).astype(BF16)
         coarse[k, gx, gy_high, gy_low, gz] = residual
         stages = coarse_stages(k)
         every_stage.extend(stages)
+        if k == 0:
+            pl.semaphore_wait(barrier, len(z_peers) + len(xy_peers))
         start(stages[0])
+        pack_faces(e, field)
+        if k == 0:
+            prepare()
+        else:
+            add_products(0)
         for i in range(own_blocks):
             if k == 0:
                 factor_loads[i].wait()
-            values = dot(factor[pl.ds(i * blk, blk), pl.ds(0, (i + 1) * blk)], own[pl.ds(0, (i + 1) * blk), :])
+            values = dot(
+                factor[pl.ds(i * blk, blk), pl.ds(0, (i + 1) * blk)],
+                own[pl.ds(0, (i + 1) * blk), :],
+            )
             front[:, pl.ds(i * blk, blk)] = values.T.astype(BF16)
-        arrive(stages[0])
-        start(stages[1])
-        for j in range(own_blocks):
-            back[:, pl.ds(j * blk, blk)] = dot(
-                front[:, pl.ds(j * blk, rows - j * blk)],
-                factor[pl.ds(j * blk, rows - j * blk), pl.ds(j * blk, blk)],
-            )
-        arrive(stages[1])
-        start(stages[2])
+            if i == own_blocks // 2 - 1:
+                arrive(stages[0])
+                start(stages[1])
         if k == 0:
             for i in range(own_blocks, all_blocks):
                 factor_loads[i].wait()
@@ -264,59 +263,70 @@
                 face_factor[pl.ds(i * blk - rows, blk), :], margin_faces
             )
             front[:, pl.ds(i * blk, blk)] = values.T.astype(BF16)
-        arrive(stages[2])
-        start(stages[3])
         for j in range(own_blocks):
-            back[:, pl.ds(j * blk, blk)] += dot(
-                front[:, pl.ds(rows, size - rows)],
-                factor[pl.ds(rows, size - rows), pl.ds(j * blk, blk)],
-            )
+            cut = pl.ds(j * blk, blk)
+            back[cut, :] = dot(
+                front[:, pl.ds(j * blk, size - j * blk)], factor[pl.ds(j * blk, size - j * blk), cut]
+            ).T
         if k == 0:
             loads[2].wait()
-        arrive(stages[3])
-        solved = dot(inverse[...], coarse[k].reshape(-1, coarse.shape[-1]))
-        solved = solved.T.astype(BF16)
-        for j in range(own_blocks):
-            cut = pl.ds(j * blk, blk)
-            search[k, cut, :] = (back[:, cut] + dot(solved, placed_basis[:, cut])).T
+        arrive(stages[1])
+        start(stages[2])
+        arrive(stages[2])
+        solved = dot(inverse[...], coarse[k].reshape(-1, coarse.shape[-1])).astype(BF16)
+        search[k] = back[...] + dot(placed_turned[...], solved)
+
+    def shaped(values):
+        return values.reshape(cy, cz, -1)
 
     def operate(k, e):
-        field = search.at[k]
+        zi = lax.broadcasted_iota(jnp.int32, (cy, cz, right.shape[1]), 1)
+        nothing = jnp.zeros((1, cz, right.shape[1]), F32)
+        result = images.at[k]
+        for c in range(comps):
+            base = c * slab
+            for x in range(cx):
+                at = pl.ds(base + x * plane, plane)
+                center = shaped(search[k, at, :])
+                beside = jnp.concatenate([nothing, center[:-1]], axis=0)
+                beside += jnp.concatenate([center[1:], nothing], axis=0)
+                beside += jnp.where(zi == 0, 0.0, pltpu.roll(center, 1, axis=1))
+                beside += jnp.where(zi == cz - 1, 0.0, pltpu.roll(center, cz - 1, axis=1))
+                if x:
+                    beside += shaped(search[k, pl.ds(base + (x - 1) * plane, plane), :])
+                if x < cx - 1:
+                    beside += shaped(search[k, pl.ds(base + (x + 1) * plane, plane), :])
+                out = shaped(diagonal[at, :]) * center - beside
+                result[at, :] = out.reshape(plane, -1)
         wait_faces(e)
-        zi = lax.broadcasted_iota(jnp.int32, (cy, cz, right.shape[1]), 1)
-        totals = None
         for c in range(comps):
             base = c * slab
             cut = pl.ds(c * plane, plane)
             x_low, x_high, y_low, y_high, z_low, z_high = (
                 faces[e, f, cut, :].astype(F32) for f in range(6)
             )
-            zpad[pl.ds(base, cx * cy, stride=cz), :] = z_low
-            zpad[pl.ds(base + cz - 1, cx * cy, stride=cz), :] = z_high
-            for x in range(cx):
-                at = pl.ds(base + x * plane, plane)
-                flat = field[at, :]
-                center = flat.reshape(cy, cz, -1)
-                lower = field[pl.ds(base + (x - 1) * plane, plane), :] if x else x_low
-                upper = field[pl.ds(base + (x + 1) * plane, plane), :] if x < cx - 1 else x_high
-                edge = zpad[at, :].reshape(cy, cz, -1)
-                beside = (lower + upper).reshape(cy, cz, -1)
-                beside += jnp.concatenate([y_low[x * cz : (x + 1) * cz][None], center[:-1]], axis=0)
-                beside += jnp.concatenate([center[1:], y_high[x * cz : (x + 1) * cz][None]], axis=0)
-                beside += jnp.where(zi == 0, edge, pltpu.roll(center, 1, axis=1))
-                beside += jnp.where(zi == cz - 1, edge, pltpu.roll(center, cz - 1, axis=1))
-                out = diagonal[at, :].reshape(cy, cz, -1) * center - beside
-                given = right[at, :].reshape(cy, cz, -1)
-                if k == 0:
-                    flat_out = out.reshape(plane, -1)
-                    image[at, :] = flat_out
-                    own[at, :] = flat_out.astype(BF16)
-                    terms = [given * given, out * given, out * out]
-                else:
-                    first = image[at, :].reshape(cy, cz, -1)
-                    terms = [out * given, out * first, out * out]
-                terms = [jnp.sum(term, axis=0) for term in terms]
-                totals = terms if totals is None else [a + b for a, b in zip(totals, terms)]
+            for z, piece in ((0, z_low), (cz - 1, z_high)):
+                result[pl.ds(base + z, cx * cy, stride=cz), :] -= piece
+            for x, piece in ((0, x_low), (cx - 1, x_high)):
+                result[pl.ds(base + x * plane, plane), :] -= piece
+            for y, piece in ((0, y_low), (cy - 1, y_high)):
+                for x in range(cx):
+                    result[pl.ds(base + x * plane + y * cz, cz), :] -= piece[x * cz : (x + 1) * cz]
+        if k == 0:
+            own[...] = result[...].astype(BF16)
+
+    def add_products(k):
+        totals = None
+        for i in range(comps * cx):
+            at = pl.ds(i * plane, plane)
+            given, first = right[at, :], images[0, at, :]
+            if k == 0:
+                terms = [given * given, first * given, first * first]
+            else:
+                second = images[1, at, :]
+                terms = [second * given, second * first, second * second]
+            terms = [jnp.sum(shaped(term), axis=0) for term in terms]
+            totals = terms if totals is None else [a + b for a, b in zip(totals, terms)]
         for q, total in enumerate(totals):
             sums_z[gz, pl.ds(k * 3 + q, 1), :] = jnp.sum(total, axis=0, keepdims=True)
 
@@ -327,15 +337,19 @@
     placed_basis[...] = dot(table, basis[...]).astype(BF16)
     loads[0].wait()
     own[...] = right[...].astype(BF16)
-    pl.semaphore_wait(barrier, len(z_peers) + len(xy_peers))
-    pack_faces(0, right)
-    precondition(0, 0)
+    outs = [
+        pltpu.make_async_copy(search.at[k], target, out_sem.at[k])
+        for k, target in enumerate((search_one_hbm, search_two_hbm))
+    ]
+    precondition(0, 0, right)
     pack_faces(1, search.at[0])
+    outs[0].start()
     operate(0, 1)
-    pack_faces(2, image)
-    precondition(1, 2)
+    precondition(1, 2, images.at[0])
     pack_faces(3, search.at[1])
+    outs[1].start()
     operate(1, 3)
+    add_products(1)
 
     sum_copies = []
 
@@ -396,10 +410,13 @@
     sine_two = norm_three / radius_two
     coef_two = -cosine_two * sine_one * start_norm / radius_two
     coef_one = (cosine_one * start_norm - turned_one * coef_two) / radius_one
-    ratio_ref[...] = sine_one * sine_two
     weight_two = coef_two / scale
     weight_one = coef_one / start_norm - along_one * weight_two
-    solution_ref[...] = weight_one * search[0] + weight_two * search[1]
+    weights_ref[0:1, :] = weight_one
+    weights_ref[1:2, :] = weight_two
+    weights_ref[2:3, :] = sine_one * sine_two
+    for out in outs:
+        out.wait()
 
     for stage in every_stage + [sum_copies]:
         for copy in stage:
@@ -410,6 +427,11 @@
             @pl.when(present[f])
             def _():
                 face_copy(e, f).wait_send()
+
+
+def combine(weights_ref, one_ref, two_ref, solution_ref, ratio_ref):
+    solution_ref[...] = weights_ref[0:1, :] * one_ref[...] + weights_ref[1:2, :] * two_ref[...]
+    ratio_ref[...] = weights_ref[2:3, :]
 
 
 def local(dims, right_side, stiffness, local_factor, basis, coarse_map, margin_index, coarse_inverse):
@@ -424,18 +446,19 @@
     assert cx == cy == cz and rows % 256 == 0 and size % 256 == 0
     low_count = 2 if dims[1] % 2 == 0 else 1
     devices = dims[0] * dims[1] * dims[2]
-    copies = sum(n - 1 for n in (dims[2], dims[0], dims[1] // low_count, low_count))
+    copies = dims[2] - 1 + dims[0] * dims[1] // low_count - 1 + low_count - 1
     sum_copies = dims[2] - 1 + dims[0] * dims[1] - 1
     anywhere = pl.BlockSpec(memory_space=pl.ANY)
     vmem = pl.BlockSpec(memory_space=pltpu.VMEM)
-    solved, ratio = pl.pallas_call(
+    search_one, search_two, weights = pl.pallas_call(
         functools.partial(kernel, dims, cells),
         out_shape=(
             jax.ShapeDtypeStruct((rows, rhs), F32),
-            jax.ShapeDtypeStruct((1, rhs), F32),
+            jax.ShapeDtypeStruct((rows, rhs), F32),
+            jax.ShapeDtypeStruct((8, rhs), F32),
         ),
         in_specs=[anywhere, vmem, anywhere, anywhere, vmem, vmem, anywhere],
-        out_specs=(vmem, vmem),
+        out_specs=(anywhere, anywhere, vmem),
         scratch_shapes=[
             pltpu.VMEM((rows, rhs), F32),
             pltpu.VMEM((size, size), BF16),
@@ -443,14 +466,14 @@
             pltpu.VMEM(coarse_inverse.shape, BF16),
             pltpu.VMEM((rows, rhs), BF16),
             pltpu.VMEM((functions, rows), BF16),
+            pltpu.VMEM((rows, functions), BF16),
             pltpu.VMEM((6 * face, margin), BF16),
             pltpu.VMEM((margin, 6 * face), BF16),
             pltpu.VMEM((rows, rhs), F32),
             pltpu.VMEM((2, rows, rhs), F32),
+            pltpu.VMEM((2, rows, rhs), F32),
+            pltpu.VMEM((rhs, size), BF16),
             pltpu.VMEM((rows, rhs), F32),
-            pltpu.VMEM((rows, rhs), F32),
-            pltpu.VMEM((rhs, size), BF16),
-            pltpu.VMEM((rhs, rows), F32),
             pltpu.VMEM((4, 6, face, rhs), BF16),
             pltpu.VMEM((4, 6, face, rhs), BF16),
             pltpu.VMEM(
@@ -466,6 +489,7 @@
             pltpu.SemaphoreType.DMA((2, copies)),
             pltpu.SemaphoreType.DMA((sum_copies,)),
             pltpu.SemaphoreType.DMA((sum_copies,)),
+            pltpu.SemaphoreType.DMA((2,)),
         ],
         compiler_params=pltpu.CompilerParams(
             collective_id=0, has_side_effects=True, vmem_limit_bytes=56 * 1024 * 1024
@@ -479,6 +503,18 @@
         margin_index.reshape(1, margin),
         coarse_inverse,
     )
+    parts = 2
+    block = pl.BlockSpec((rows // parts, rhs), lambda i: (i, 0))
+    solved, ratio = pl.pallas_call(
+        combine,
+        grid=(parts,),
+        out_shape=(
+            jax.ShapeDtypeStruct((rows, rhs), F32),
+            jax.ShapeDtypeStruct((1, rhs), F32),
+        ),
+        in_specs=[pl.BlockSpec((8, rhs), lambda i: (0, 0)), block, block],
+        out_specs=(block, pl.BlockSpec((1, rhs), lambda i: (0, 0))),
+    )(weights, search_one, search_two)
     return solved.reshape(right_side.shape), ratio.reshape(rhs)
 
 

time: 54.1 us -> 44.7 us (0.83)
  Pallas kernels: 50.1 us -> 43.9 us
  local copies, waits for them, and re-layouts: 3.17 us -> 0 us
    pallas_call x1, Pallas kernels: 50.1 us -> 41.7 us  [local(): pl.pallas_call(functools.partial(kernel, dims, cells), out_shape=(jax.Sha...]
    unnamed x2 -> x0, local copies, waits for them, and re-layouts: 3.17 us -> none
    pallas_call x0 -> x1, Pallas kernels: none -> 2.17 us  [local(): pl.pallas_call(combine, grid=(parts,), out_shape=(jax.ShapeDtypeStruct((r...]
where the time goes in v2:
time: 44.7 us; the launch traced here: 44.5 us
  Pallas kernels  43.9 us (98%)
  between operations  0.64 us (1%)
    pallas_call x1, Pallas kernels, local(): pl.pallas_call(functools.partial(kernel, dims, cells), out_shape=(jax.Sha...  41.7 us
    pallas_call x1, Pallas kernels, local(): pl.pallas_call(combine, grid=(parts,), out_shape=(jax.ShapeDtypeStruct((r...  2.17 us

profile of v2, /device:TPU:0, one launch (start us, length us, event | category | flops | bytes accessed | tf_op | source)
XLA Modules:
  0.0 44.5 jit_solution(10770058370181163795)
XLA Ops:
  0.6 41.7 %shard_map.86 = (f32[1536,128]{1,0:T(8,128)}, f32[1536,128]{1,0:T(8,128)}, f32[8,128]{1,0:T(8,128)}) custom-call(f32[1536,128]{1,0:T(8,128)} %bitcast.9, f32[24,8,8]{2,1,0:T(8,128)} %bitcast.11, bf16[2048,2048]{1,0:T(8,128)(2,1)} %bitcast.8, bf16[64,1536]{1,0:T(8,128)(2,1)} %bitcast.10, s32[1,64]{1,0:T(1,128)} %bitcast.13, s32[1,512]{1,0:T(1,128)} %bitcast.12, ...), custom_call_target="tpu_custom_call" | custom-call | tf_op jit(solution)/shard_map/pallas_call | solution.py:453
  42.3 2.2 %shard_map.87 = (f32[1536,128]{1,0:T(8,128)}, f32[1,128]{1,0:T(1,128)}) custom-call(f32[8,128]{1,0:T(8,128)} %get-tuple-element.7.weights_ref, f32[1536,128]{1,0:T(8,128)} %get-tuple-element.8.one_ref, f32[1536,128]{1,0:T(8,128)} %get-tuple-element.9.two_ref), custom_call_target="tpu_custom_call" | custom-call | tf_op jit(solution)/shard_map/pallas_call | solution.py:508
